TPU v7x, 32 devices: a whole 2x2x4 slice. The times are simulated.
32 devices in a mesh: seq: 8 (over z, y), head: 4 (over x, core).
Axes of the slice: x: 2, y: 2, z: 4, core: 2. Of those that a mesh axis runs over, the one named last changes fastest.
Arguments:
- layer_input: bfloat16 [4, 1024, 8192], P('head', 'seq'), may hold values from -6 to 6
- out_grad: bfloat16 [4, 1024, 8192], P('head', 'seq'), may hold values from -6 to 6
- attention_out: bfloat16 [4, 1024, 4096], P('head', 'seq'), may hold values from -6 to 6
- frozen_output_grad: bfloat16 [4, 1024, 4096], P('head', 'seq'), may hold values from -6 to 6
- query_rows: bfloat16 [4, 1024, 4096], P('head', 'seq'), may hold values from -120 to 120
- key_rows: bfloat16 [4, 1024, 512], P('head', 'seq'), may hold values from -4 to 4
- value_rows: bfloat16 [4, 1024, 512], P('head', 'seq'), may hold values from -6 to 6
- seg_lengths: int32 [4, 8], P('head'), may hold values from 1 to 256, 1024 in all within a row
- use_list: int32 [4, 8], replicated, may hold values from 0 to 31, as said below
- store_map: int32 [32], replicated, may hold values from 0 to 31, as said below
- query_down: float32 [32, 64, 8192], P('head', None, 'seq'), may hold values from -0.0625 to 0.0625
- query_up: float32 [32, 64, 4096], P('head', None, 'seq'), may hold values from -0.75 to 0.75
- output_down: float32 [32, 64, 4096], P('head', None, 'seq'), may hold values from -0.09375 to 0.09375
- output_up: float32 [32, 64, 8192], P('head', None, 'seq'), may hold values from -0.75 to 0.75
Outputs:
- grad_query_down: float32 [32, 64, 8192], P('head', None, 'seq')
- grad_query_up: float32 [32, 64, 4096], P('head', None, 'seq')
- grad_output_down: float32 [32, 64, 4096], P('head', None, 'seq')
- grad_output_up: float32 [32, 64, 8192], P('head', None, 'seq')
Inputs may be any that keep to these rules, and one draw needn't show every extreme that they name: `use_list`: each row names 8 distinct tenants. Counting a tenant's store index as store_map[tenant] // 8, a row names at most 2 tenants of one store index, and exactly 2 of some store index in every row. A permutation: tenant t's adapters are in slot store_map[t]. `seg_lengths`: each row sums to 1024.
All inputs are finite; a program needn't handle non-finite values.
Results may differ from a plain program's by a relative error of at most 0.024.
Values may be sent and summed in bfloat16 or wider, within the bound.
A program may use at most 128 MiB of HBM per device.

v0:
```python
import math
import jax
import jax.numpy as jnp
from jax import lax
from jax.sharding import PartitionSpec as P

QH = 32
KVH = 4
HD = 128
CAP = 2
adapter_scale = 2.0
big_negative = -1e30
highest = lax.Precision.HIGHEST


def contract_axes(left_side, right_side, left_dim, right_dim):
    return lax.dot_general(
        left_side,
        right_side,
        (((left_dim,), (right_dim,)), ((), ())),
        preferred_element_type=jnp.float32,
    )


def narrow(full_rows, tenant_row_mask, rank_size):
    length, used_count = tenant_row_mask.shape
    return jnp.sum(
        full_rows.reshape(length, used_count, rank_size) * tenant_row_mask[:, :, None], axis=1
    )


def widened_rows(low_rows, tenant_row_mask):
    length, used_count = tenant_row_mask.shape
    spread_rows = tenant_row_mask.astype(jnp.bfloat16)[:, :, None] * low_rows[:, None, :]
    return spread_rows.reshape(length, used_count * low_rows.shape[1])


def request_tables(use_list, store_map, slots_dev):
    tenants = store_map.shape[0]
    used_count = use_list.shape[1]
    matches = use_list[:, :, None] == jnp.arange(tenants, dtype=jnp.int32)[None, None, :]
    slot_index = jnp.sum(jnp.where(matches, store_map[None, None, :], 0), axis=2)
    owner_index = slot_index // slots_dev
    local_slot = slot_index % slots_dev
    same_owner = (owner_index[:, :, None] == owner_index[:, None, :]).astype(jnp.int32)
    indices = jnp.arange(used_count, dtype=jnp.int32)
    earlier = (indices[None, :] < indices[:, None]).astype(jnp.int32)
    rank_index = jnp.sum(same_owner * earlier[None, :, :], axis=2)
    return (owner_index, local_slot, rank_index)


def attention_grad(query_heads, key_heads, value_heads, gradient_heads, segment, key_span):
    length, head_count, head_width = query_heads.shape
    block_rows = min(512, length)
    window = block_rows + key_span
    factor = 1.0 / math.sqrt(head_width)
    padded_keys = jnp.pad(key_heads, ((key_span, 0), (0, 0), (0, 0)))
    padded_values = jnp.pad(value_heads, ((key_span, 0), (0, 0), (0, 0)))
    padded_segment = jnp.concatenate([jnp.full((key_span,), -1, jnp.int32), segment])

    def one_block(row_start):
        query_block = lax.dynamic_slice_in_dim(query_heads, row_start, block_rows, 0)
        grad_block = lax.dynamic_slice_in_dim(gradient_heads, row_start, block_rows, 0)
        key_block = lax.dynamic_slice_in_dim(padded_keys, row_start, window, 0)
        value_block = lax.dynamic_slice_in_dim(padded_values, row_start, window, 0)
        query_segment = lax.dynamic_slice_in_dim(segment, row_start, block_rows, 0)
        key_segment = lax.dynamic_slice_in_dim(padded_segment, row_start, window, 0)
        query_pos = row_start + jnp.arange(block_rows, dtype=jnp.int32)
        key_pos = row_start - key_span + jnp.arange(window, dtype=jnp.int32)
        allowed = (query_segment[:, None] == key_segment[None, :]) & (
            key_pos[None, :] <= query_pos[:, None]
        )
        scores = (
            jnp.einsum("qhd,khd->hqk", query_block, key_block, preferred_element_type=jnp.float32)
            * factor
        )
        scores = jnp.where(allowed[None, :, :], scores, big_negative)
        row_max = jnp.max(scores, axis=2, keepdims=True)
        weights = jnp.exp(scores - row_max)
        probabilities = weights / jnp.sum(weights, axis=2, keepdims=True)
        prob_grad = jnp.einsum(
            "qhd,khd->hqk", grad_block, value_block, preferred_element_type=jnp.float32
        )
        inner = jnp.sum(probabilities * prob_grad, axis=2, keepdims=True)
        score_grad = (probabilities * (prob_grad - inner)).astype(jnp.bfloat16)
        query_gradient = (
            jnp.einsum("hqk,khd->qhd", score_grad, key_block, preferred_element_type=jnp.float32)
            * factor
        )
        return query_gradient.astype(jnp.bfloat16)

    starts = jnp.arange(0, length, block_rows, dtype=jnp.int32)
    return lax.map(one_block, starts).reshape(length, head_count * head_width)


def shards(
    layer_input,
    out_grad,
    attention_out,
    frozen_output_grad,
    query_rows,
    key_rows,
    value_rows,
    seg_lengths,
    use_list,
    store_map,
    query_down,
    query_up,
    output_down,
    output_up,
):
    slots_dev = query_down.shape[0]
    rank_size = query_down.shape[1]
    group_size = QH // KVH
    input_columns, gradient_columns, head_outputs, base_heads, query_heads = (
        lax.all_to_all(layer_input[0], "seq", split_axis=1, concat_axis=0, tiled=True),
        lax.all_to_all(out_grad[0], "seq", split_axis=1, concat_axis=0, tiled=True),
        lax.all_to_all(attention_out[0], "seq", split_axis=1, concat_axis=0, tiled=True),
        lax.all_to_all(frozen_output_grad[0], "seq", split_axis=1, concat_axis=0, tiled=True),
        lax.all_to_all(query_rows[0], "seq", split_axis=1, concat_axis=0, tiled=True),
    )
    length = input_columns.shape[0]
    heads_here = query_heads.shape[1] // HD
    first_head = lax.axis_index("seq") * heads_here
    gathered_keys, gathered_values = (
        lax.all_gather(key_rows[0], "seq", axis=0, tiled=True),
        lax.all_gather(value_rows[0], "seq", axis=0, tiled=True),
    )
    kv_index = (first_head + jnp.arange(heads_here, dtype=jnp.int32)) // group_size
    key_heads = jnp.take(gathered_keys.reshape(length, KVH, HD), kv_index, axis=1)
    value_heads = jnp.take(gathered_values.reshape(length, KVH, HD), kv_index, axis=1)
    owner_index, local_slot, rank_index = request_tables(use_list, store_map, slots_dev)
    my_index = lax.axis_index("head")
    batch_count = use_list.shape[0]
    cap_ids = jnp.arange(CAP, dtype=jnp.int32)
    slot_ids = jnp.arange(slots_dev, dtype=jnp.int32)
    matched = (
        (owner_index == my_index)[:, :, None, None]
        & (rank_index[:, :, None, None] == cap_ids[None, None, :, None])
        & (local_slot[:, :, None, None] == slot_ids[None, None, None, :])
    )
    select = jnp.sum(matched.astype(jnp.float32), axis=1)

    def pack_slots(store_part):
        return jnp.einsum("mcl,lrw->mcrw", select, store_part, precision=highest).astype(
            jnp.bfloat16
        )

    fetched = (
        lax.all_to_all(pack_slots(query_down), "head", split_axis=0, concat_axis=0, tiled=True),
        lax.all_to_all(pack_slots(query_up), "head", split_axis=0, concat_axis=0, tiled=True),
        lax.all_to_all(pack_slots(output_down), "head", split_axis=0, concat_axis=0, tiled=True),
        lax.all_to_all(pack_slots(output_up), "head", split_axis=0, concat_axis=0, tiled=True),
    )
    mine_owner = lax.dynamic_index_in_dim(owner_index, my_index, 0, keepdims=False)
    mine_rank = lax.dynamic_index_in_dim(rank_index, my_index, 0, keepdims=False)
    store_ids = jnp.arange(batch_count, dtype=jnp.int32)
    picker = (
        (mine_owner[:, None, None] == store_ids[None, :, None])
        & (mine_rank[:, None, None] == cap_ids[None, None, :])
    ).astype(jnp.float32)
    picker_half = picker.astype(jnp.bfloat16)

    def unpack(received):
        chosen = jnp.einsum(
            "ijc,jcrw->irw", picker_half, received, preferred_element_type=jnp.float32
        ).astype(jnp.bfloat16)
        return chosen.reshape(chosen.shape[0] * chosen.shape[1], chosen.shape[2])

    flattened_list = [unpack(received) for received in fetched]
    lengths = seg_lengths[0]
    used_count = lengths.shape[0]
    offsets = jnp.cumsum(lengths) - lengths
    positions = jnp.arange(length, dtype=jnp.int32)
    segment = jnp.sum((positions[:, None] >= offsets[None, :]).astype(jnp.int32), axis=1) - 1
    tenant_row_mask = (segment[:, None] == jnp.arange(used_count, dtype=jnp.int32)[None, :]).astype(
        jnp.float32
    )
    partial_out = narrow(
        contract_axes(head_outputs, flattened_list[2], 1, 1), tenant_row_mask, rank_size
    )
    partial_grad = narrow(
        contract_axes(gradient_columns, flattened_list[3], 1, 1), tenant_row_mask, rank_size
    )
    partial_query = narrow(
        contract_axes(input_columns, flattened_list[0], 1, 1), tenant_row_mask, rank_size
    )
    summed_out, summed_grad, summed_query = (
        lax.psum(partial_out.astype(jnp.bfloat16), "seq").astype(jnp.float32),
        lax.psum(partial_grad.astype(jnp.bfloat16), "seq").astype(jnp.float32),
        lax.psum(partial_query.astype(jnp.bfloat16), "seq").astype(jnp.float32),
    )
    low_rank_output = summed_out.astype(jnp.bfloat16)
    low_grad = summed_grad.astype(jnp.bfloat16)
    low_rank_query = summed_query.astype(jnp.bfloat16)
    widened_gradient = widened_rows(low_grad, tenant_row_mask)
    gradient_heads = (
        base_heads.astype(jnp.float32)
        + adapter_scale
        * jnp.dot(widened_gradient, flattened_list[2], preferred_element_type=jnp.float32)
    ).astype(jnp.bfloat16)
    query_gradient = attention_grad(
        query_heads.reshape(length, heads_here, HD),
        key_heads,
        value_heads,
        gradient_heads.reshape(length, heads_here, HD),
        segment,
        length // 4,
    )
    partial_back = narrow(
        contract_axes(query_gradient, flattened_list[1], 1, 1), tenant_row_mask, rank_size
    )
    low_rank_back = lax.psum(partial_back.astype(jnp.bfloat16), "seq")
    outer_products = (
        adapter_scale
        * contract_axes(widened_rows(low_rank_back, tenant_row_mask), input_columns, 0, 0),
        adapter_scale
        * contract_axes(widened_rows(low_rank_query, tenant_row_mask), query_gradient, 0, 0),
        adapter_scale * contract_axes(widened_gradient, head_outputs, 0, 0),
        adapter_scale
        * contract_axes(widened_rows(low_rank_output, tenant_row_mask), gradient_columns, 0, 0),
    )

    def spread(gradient):
        pieces = gradient.reshape(used_count, rank_size, gradient.shape[1])
        return jnp.einsum("ijc,irw->jcrw", picker, pieces, precision=highest)

    returned = (
        lax.all_to_all(
            spread(outer_products[0]).astype(jnp.bfloat16),
            "head",
            split_axis=0,
            concat_axis=0,
            tiled=True,
        ).astype(jnp.float32),
        lax.all_to_all(
            spread(outer_products[1]).astype(jnp.bfloat16),
            "head",
            split_axis=0,
            concat_axis=0,
            tiled=True,
        ).astype(jnp.float32),
        lax.all_to_all(
            spread(outer_products[2]).astype(jnp.bfloat16),
            "head",
            split_axis=0,
            concat_axis=0,
            tiled=True,
        ).astype(jnp.float32),
        lax.all_to_all(
            spread(outer_products[3]).astype(jnp.bfloat16),
            "head",
            split_axis=0,
            concat_axis=0,
            tiled=True,
        ).astype(jnp.float32),
    )

    def settle(received):
        return jnp.einsum("mcl,mcrw->lrw", select, received, precision=highest)

    return (settle(returned[0]), settle(returned[1]), settle(returned[2]), settle(returned[3]))


def solution(mesh):
    placed = (
        P("head", "seq", None),
        P("head", "seq", None),
        P("head", "seq", None),
        P("head", "seq", None),
        P("head", "seq", None),
        P("head", "seq", None),
        P("head", "seq", None),
        P("head", None),
        P(),
        P(),
        P("head", None, "seq"),
        P("head", None, "seq"),
        P("head", None, "seq"),
        P("head", None, "seq"),
    )
    return jax.shard_map(
        shards,
        mesh=mesh,
        in_specs=placed,
        out_specs=(
            P("head", None, "seq"),
            P("head", None, "seq"),
            P("head", None, "seq"),
            P("head", None, "seq"),
        ),
        check_vma=False,
    )
```

profile of v0, /device:TPU:0, one launch (start us, length us, event | category | flops | bytes accessed | tf_op | source)
XLA Modules:
  0.0 579.0 jit_solution(9823844953946376288)
XLA Ops:
  13.1 4.2 all-to-all-start.4
  20.1 6.7 %all-to-all-done.4 = bf16[4,2,64,512]{3,1,2,0:T(2,128)(2,1)} async-done(((bf16[4,2,64,512]{3,1,2,0:T(2,128)(2,1)}), bf16[4,2,64,512]{3,1,2,0:T(2,128)(2,1)}, u32[]{:S(2)}, u32[]{:S(2)}) %all-to-all-start.4) | async-done | bytes 524320 | tf_op jit(solution)/shard_map/all_to_all | solution.py:152
  43.5 5.4 fusion.34
  50.7 7.2 %all-to-all-done.2 = bf16[4,2,64,1024]{3,1,2,0:T(2,128)(2,1)S(1)} async-done(((bf16[4,2,64,1024]{3,1,2,0:T(2,128)(2,1)}), bf16[4,2,64,1024]{3,1,2,0:T(2,128)(2,1)S(1)}, u32[]{:S(2)}, u32[]{:S(2)}) %all-to-all-start.2) | async-done | bytes 1048608 | tf_op jit(solution)/shard_map/all_to_all | solution.py:153
  63.8 13.1 %all-to-all-done.8 = bf16[4,2,64,1024]{3,1,2,0:T(2,128)(2,1)S(1)} async-done(((bf16[4,2,64,1024]{3,1,2,0:T(2,128)(2,1)}), bf16[4,2,64,1024]{3,1,2,0:T(2,128)(2,1)S(1)}, u32[]{:S(2)}, u32[]{:S(2)}) %all-to-all-start.8) | async-done | bytes 1048608 | tf_op jit(solution)/shard_map/all_to_all | solution.py:150
  77.8 6.7 %all-to-all-start.10 = ((bf16[128,8,512]{0,2,1:T(8,128)(2,1)}), bf16[128,8,512]{0,2,1:T(8,128)(2,1)S(1)}, u32[]{:S(2)}, u32[]{:S(2)}) async-start(bf16[128,8,512]{0,2,1:T(8,128)(2,1)} %bitcast.60), calls=%async_computation.10 | async-start | bytes 2097152 | tf_op jit(solution)/shard_map/all_to_all | solution.py:118
  85.8 24.3 %all-to-all-done.10 = bf16[128,8,512]{0,2,1:T(8,128)(2,1)S(1)} async-done(((bf16[128,8,512]{0,2,1:T(8,128)(2,1)}), bf16[128,8,512]{0,2,1:T(8,128)(2,1)S(1)}, u32[]{:S(2)}, u32[]{:S(2)}) %all-to-all-start.10) | async-done | bytes 1048608 | tf_op jit(solution)/shard_map/all_to_all | solution.py:118
  117.8 21.8 %all-to-all-done = bf16[128,8,512]{0,2,1:T(8,128)(2,1)S(1)} async-done(((bf16[128,8,512]{0,2,1:T(8,128)(2,1)}), bf16[128,8,512]{0,2,1:T(8,128)(2,1)S(1)}, u32[]{:S(2)}, u32[]{:S(2)}) %all-to-all-start) | async-done | bytes 1048608 | tf_op jit(solution)/shard_map/all_to_all | solution.py:120
  149.1 52.8 %all-to-all-done.3 = bf16[128,8,1024]{0,2,1:T(8,128)(2,1)S(1)} async-done(((bf16[128,8,1024]{0,2,1:T(8,128)(2,1)}), bf16[128,8,1024]{0,2,1:T(8,128)(2,1)S(1)}, u32[]{:S(2)}, u32[]{:S(2)}) %all-to-all-start.3) | async-done | bytes 2097184 | tf_op jit(solution)/shard_map/all_to_all | solution.py:117
  203.2 4.4 all-to-all-start.6
  217.7 47.6 %all-to-all-done.6 = bf16[128,8,1024]{0,2,1:T(8,128)(2,1)} async-done(((bf16[128,8,1024]{0,2,1:T(8,128)(2,1)}), bf16[128,8,1024]{0,2,1:T(8,128)(2,1)}, u32[]{:S(2)}, u32[]{:S(2)}) %all-to-all-start.6) | async-done | bytes 2097184 | tf_op jit(solution)/shard_map/all_to_all | solution.py:116
  265.3 4.5 all-to-all-start.1
  303.0 65.1 %all-reduce.7.cloned.1.call-done = bf16[1024,64]{0,1:T(8,128)(2,1)} async-done(((bf16[1024,64]{0,1:T(8,128)(2,1)}), bf16[1024,64]{0,1:T(8,128)(2,1)}) %all-reduce.7.cloned.1.call-update) | async-done | bytes 131088 | tf_op jit(solution)/shard_map/psum | solution.py:190
  371.1 50.4 %while.12 = (s32[]{:T(128)}, bf16[2,512,4,128]{3,2,1,0:T(4,128)(2,1)}, s32[2]{0:T(128)S(1)}, bf16[1280,4,128]{2,0,1:T(8,128)(2,1)S(1)}, s32[1024]{0:T(1024)S(1)}...) while((s32[]{:T(128)}, ...), condition=%wide.region_11.13_spmd, body=%wide.region_7.12_spmd.sunk | while | flops 1230110720 | bytes 50923260 | solution.py:93
  375.2 5.1 fusion.110
  382.2 7.7 %fusion.111 = (f32[4,512]{1,0:T(4,128)S(1)}, f32[4,512,768]{2,1,0:T(8,128)S(1)}) fusion(f32[4,512,768]{2,1,0:T(8,128)} %fusion.110, pred[512,768]{1,0:T(8,128)(4,1)S(1)} %compare_and_fusion.4), kind=kOutput, calls=%fused_computation.141.clone.1 | output fusion | flops 9437951 | bytes 12984320 | tf_op jit(solution)/shard_map/while/body/eval_jaxpr/sub | solution.py:79
  400.4 5.0 fusion.110
  407.3 7.7 %fusion.111 = (f32[4,512]{1,0:T(4,128)S(1)}, f32[4,512,768]{2,1,0:T(8,128)S(1)}) fusion(f32[4,512,768]{2,1,0:T(8,128)} %fusion.110, pred[512,768]{1,0:T(8,128)(4,1)S(1)} %compare_and_fusion.4), kind=kOutput, calls=%fused_computation.141.clone.1 | output fusion | flops 9437951 | bytes 12984320 | tf_op jit(solution)/shard_map/while/body/eval_jaxpr/sub | solution.py:79
  424.5 71.3 %all-reduce.9.cloned.1.call-done = (bf16[1024,64]{0,1:T(8,128)(2,1)}, bf16[1024,64]{0,1:T(8,128)(2,1)}, bf16[1024,64]{0,1:T(8,128)(2,1)}) async-done(((bf16[1024,64]{0,1:T(8,128)(2,1)}, bf16[1024,64]{0,1:T(8,128)(2,1)}, bf16[1024,64]{0,1:T(8,128)(2,1)}), (bf16[1024,64]{0,1:T(8,128)(2,1)}, bf16[1024,64]{0,1:T(8,128)(2,1)}, bf16[1024,64]{0,1:T(8,128)(2,1)})) %all-reduce.9.cloned.1.call-update) | async-done | bytes 393232 | tf_op jit(solution)/shard_map/psum | solution.py:213
  502.0 4.3 all-to-all-start.9
  510.9 4.3 all-to-all-done.9
  538.8 7.4 %all-to-all-done.12 = bf16[4,2,64,1024]{3,1,2,0:T(2,128)(2,1)S(1)} async-done(((bf16[4,2,64,1024]{3,1,2,0:T(2,128)(2,1)}), bf16[4,2,64,1024]{3,1,2,0:T(2,128)(2,1)S(1)}, u32[]{:S(2)}, u32[]{:S(2)}) %all-to-all-start.12) | async-done | bytes 1048608 | tf_op jit(solution)/shard_map/all_to_all | solution.py:250
  546.2 4.5 all-to-all-start.7
  565.2 4.3 convolution_bitcast_fusion.1
  (183 shorter events, 170.5 us)
Async XLA Ops:
  7.2 23.0 %copy-start = (f32[8,64,1024]{2,1,0:T(8,128)S(1)}, f32[8,64,1024]{2,1,0:T(8,128)}, u32[]{:S(2)}) copy-start(f32[8,64,1024]{2,1,0:T(8,128)} %param.31) | copy-start | bytes 6291460
  8.7 34.8 %copy-start.26 = (f32[4,2,8]{2,1,0:T(2,128)}, f32[4,2,8]{2,1,0:T(2,128)S(1)}, u32[]{:S(2)}) copy-start(f32[4,2,8]{2,1,0:T(2,128)S(1)} %convert_reduce_fusion.1) | copy-start | bytes 772
  13.1 13.7 %all-to-all-start.4 = ((bf16[4,2,64,512]{3,1,2,0:T(2,128)(2,1)}), bf16[4,2,64,512]{3,1,2,0:T(2,128)(2,1)}, u32[]{:S(2)}, u32[]{:S(2)}) async-start(bf16[4,2,64,512]{3,1,2,0:T(2,128)(2,1)} %copy.141), calls=%async_computation.4 | async-start | bytes 1048576 | tf_op jit(solution)/shard_map/all_to_all | solution.py:152
  26.7 12.3 %all-to-all-start.5 = ((bf16[4,2,64,512]{3,2,1,0:T(8,128)(2,1)}), bf16[4,2,64,512]{3,2,1,0:T(8,128)(2,1)S(1)}, u32[]{:S(2)}, u32[]{:S(2)}) async-start(bf16[4,2,64,512]{3,2,1,0:T(8,128)(2,1)} %copy.151), calls=%async_computation.5 | async-start | bytes 1048576 | tf_op jit(solution)/shard_map/all_to_all | solution.py:151
  39.8 18.1 %all-to-all-start.2 = ((bf16[4,2,64,1024]{3,1,2,0:T(2,128)(2,1)}), bf16[4,2,64,1024]{3,1,2,0:T(2,128)(2,1)S(1)}, u32[]{:S(2)}, u32[]{:S(2)}) async-start(bf16[4,2,64,1024]{3,1,2,0:T(2,128)(2,1)} %copy.134), calls=%async_computation.2 | async-start | bytes 2097152 | tf_op jit(solution)/shard_map/all_to_all | solution.py:153
  58.9 18.0 %all-to-all-start.8 = ((bf16[4,2,64,1024]{3,1,2,0:T(2,128)(2,1)}), bf16[4,2,64,1024]{3,1,2,0:T(2,128)(2,1)S(1)}, u32[]{:S(2)}, u32[]{:S(2)}) async-start(bf16[4,2,64,1024]{3,1,2,0:T(2,128)(2,1)} %copy.162), calls=%async_computation.8 | async-start | bytes 2097152 | tf_op jit(solution)/shard_map/all_to_all | solution.py:150
  62.5 22.1 %copy-start.11 = (bf16[1,128,4096]{2,1,0:T(8,128)(2,1)S(1)}, bf16[1,128,4096]{2,1,0:T(8,128)(2,1)}, u32[]{:S(2)}) copy-start(bf16[1,128,4096]{2,1,0:T(8,128)(2,1)} %param.22) | copy-start | bytes 3145732
  77.8 32.3 %all-to-all-start.10 = ((bf16[128,8,512]{0,2,1:T(8,128)(2,1)}), bf16[128,8,512]{0,2,1:T(8,128)(2,1)S(1)}, u32[]{:S(2)}, u32[]{:S(2)}) async-start(bf16[128,8,512]{0,2,1:T(8,128)(2,1)} %bitcast.60), calls=%async_computation.10 | async-start | bytes 2097152 | tf_op jit(solution)/shard_map/all_to_all | solution.py:118
  110.2 29.4 %all-to-all-start = ((bf16[128,8,512]{0,2,1:T(8,128)(2,1)}), bf16[128,8,512]{0,2,1:T(8,128)(2,1)S(1)}, u32[]{:S(2)}, u32[]{:S(2)}) async-start(bf16[128,8,512]{0,2,1:T(8,128)(2,1)} %bitcast.10), calls=%async_computation | async-start | bytes 2097152 | tf_op jit(solution)/shard_map/all_to_all | solution.py:120
  140.6 61.3 %all-to-all-start.3 = ((bf16[128,8,1024]{0,2,1:T(8,128)(2,1)}), bf16[128,8,1024]{0,2,1:T(8,128)(2,1)S(1)}, u32[]{:S(2)}, u32[]{:S(2)}) async-start(bf16[128,8,1024]{0,2,1:T(8,128)(2,1)} %bitcast.184), calls=%async_computation.3 | async-start | bytes 4194304 | tf_op jit(solution)/shard_map/all_to_all | solution.py:117
  144.2 131.8 %all-gather.5.cloned.1.call-start = ((), (), s32[]{:S(2)}) async-start(), calls=%async_computation.14 | async-start | bytes 1179648 | tf_op jit(solution)/shard_map/all_gather | solution.py:126
  203.2 62.1 %all-to-all-start.6 = ((bf16[128,8,1024]{0,2,1:T(8,128)(2,1)}), bf16[128,8,1024]{0,2,1:T(8,128)(2,1)}, u32[]{:S(2)}, u32[]{:S(2)}) async-start(bf16[128,8,1024]{0,2,1:T(8,128)(2,1)} %bitcast.183), calls=%async_computation.6 | async-start | bytes 4194304 | tf_op jit(solution)/shard_map/all_to_all | solution.py:116
  207.6 70.1 %all-gather.7.cloned.1.call-start = ((), (), s32[]{:S(2)}) async-start(), calls=%async_computation.15 | async-start | bytes 1179648 | tf_op jit(solution)/shard_map/all_gather | solution.py:127
  215.5 54.8 %copy-start.14 = (bf16[4,2,64,1024]{3,1,2,0:T(2,128)(2,1)S(1)}, bf16[4,2,64,1024]{3,1,2,0:T(2,128)(2,1)}, u32[]{:S(2)}) copy-start(bf16[4,2,64,1024]{3,1,2,0:T(2,128)(2,1)} %copy-done.13) | copy-start | bytes 3145732
  265.3 37.7 %all-to-all-start.1 = ((bf16[128,8,512]{0,2,1:T(8,128)(2,1)}), bf16[128,8,512]{0,2,1:T(8,128)(2,1)}, u32[]{:S(2)}, u32[]{:S(2)}) async-start(bf16[128,8,512]{0,2,1:T(8,128)(2,1)} %bitcast.12), calls=%async_computation.1 | async-start | bytes 2097152 | tf_op jit(solution)/shard_map/all_to_all | solution.py:119
  269.9 98.3 %all-reduce.7.cloned.1.call-start = ((), (), s32[]{:S(2)}) async-start(), calls=%async_computation.13 | async-start | bytes 262144 | tf_op jit(solution)/shard_map/psum | solution.py:190
  297.9 197.9 %all-reduce.9.cloned.1.call-start = ((), (), s32[]{:S(2)}) async-start(), calls=%async_computation.16 | async-start | bytes 786432 | tf_op jit(solution)/shard_map/psum | solution.py:213
  300.9 67.2 %copy-start.22 = (bf16[8,64,512]{2,0,1:T(8,128)(2,1)S(1)}, bf16[8,64,512]{2,0,1:T(8,128)(2,1)}, u32[]{:S(2)}) copy-start(bf16[8,64,512]{2,0,1:T(8,128)(2,1)} %copy-done.21) | copy-start | bytes 1572868
  423.0 72.8 %copy-start.23 = (bf16[1024,64]{0,1:T(8,128)(2,1)S(1)}, bf16[1024,64]{0,1:T(8,128)(2,1)}, u32[]{:S(2)}) copy-start(bf16[1024,64]{0,1:T(8,128)(2,1)} %all-reduce.7.cloned.1.call-done) | copy-start | bytes 393220
  502.0 13.2 %all-to-all-start.9 = ((bf16[4,2,64,512]{3,1,2,0:T(2,128)(2,1)}), bf16[4,2,64,512]{3,1,2,0:T(2,128)(2,1)}, u32[]{:S(2)}, u32[]{:S(2)}) async-start(bf16[4,2,64,512]{3,1,2,0:T(2,128)(2,1)} %copy.166), calls=%async_computation.9 | async-start | bytes 1048576 | tf_op jit(solution)/shard_map/all_to_all | solution.py:236
  515.2 13.0 %all-to-all-start.11 = ((bf16[4,2,64,512]{3,1,2,0:T(2,128)(2,1)}), bf16[4,2,64,512]{3,1,2,0:T(2,128)(2,1)}, u32[]{:S(2)}, u32[]{:S(2)}) async-start(bf16[4,2,64,512]{3,1,2,0:T(2,128)(2,1)} %copy.172), calls=%async_computation.11 | async-start | bytes 1048576 | tf_op jit(solution)/shard_map/all_to_all | solution.py:243
  528.3 18.0 %all-to-all-start.12 = ((bf16[4,2,64,1024]{3,1,2,0:T(2,128)(2,1)}), bf16[4,2,64,1024]{3,1,2,0:T(2,128)(2,1)S(1)}, u32[]{:S(2)}, u32[]{:S(2)}) async-start(bf16[4,2,64,1024]{3,1,2,0:T(2,128)(2,1)} %copy.177), calls=%async_computation.12 | async-start | bytes 2097152 | tf_op jit(solution)/shard_map/all_to_all | solution.py:250
  537.1 13.7 %copy-start.27 = (f32[4,2,8]{2,1,0:T(2,128)S(1)}, f32[4,2,8]{2,1,0:T(2,128)}, u32[]{:S(2)}) copy-start(f32[4,2,8]{2,1,0:T(2,128)} %copy-done.26) | copy-start | bytes 772
  546.2 19.0 %all-to-all-start.7 = ((bf16[4,2,64,1024]{3,1,2,0:T(2,128)(2,1)}), bf16[4,2,64,1024]{3,1,2,0:T(2,128)(2,1)}, u32[]{:S(2)}, u32[]{:S(2)}) async-start(bf16[4,2,64,1024]{3,1,2,0:T(2,128)(2,1)} %copy.157), calls=%async_computation.7 | async-start | bytes 2097152 | tf_op jit(solution)/shard_map/all_to_all | solution.py:229
  (23 other events, 106.6 us)
Sparse Core Ops, SparseCore 0:
  147.1 61.6 all-gather.4
  210.9 61.0 all-gather.6
  298.0 70.0 all-reduce.6
  424.6 71.1 all-reduce.8
where the time goes:
time: 588 us; the launch traced here: 579 us
  waiting for transfers between devices  329 us (56%)
  matrix products  79.1 us (13%)
  local copies, waits for them, and re-layouts  67.7 us (12%)
  starting transfers between devices  54.7 us (9%)
  other arithmetic  25.2 us (4%)
  between operations  14.8 us (3%)
  loops' own time  8.21 us (1%)
    psum x1, waiting for transfers between devices, shards(): low_rank_back = lax.psum(partial_back.astype(jnp.bfloat16), 'seq')  71.3 us
    psum x1, waiting for transfers between devices, shards(): lax.psum(partial_grad.astype(jnp.bfloat16), 'seq').astype(jnp.float32)  65.1 us
    all_to_all x1, waiting for transfers between devices, shards(): lax.all_to_all(out_grad[0], 'seq', split_axis=1, concat_axis=0, tiled=True)  52.8 us
    all_to_all x1, waiting for transfers between devices, shards(): lax.all_to_all(layer_input[0], 'seq', split_axis=1, concat_axis=0, tiled=...  47.6 us
    unnamed x71, local copies, waits for them, and re-layouts  28.1 us
    all_to_all x1, waiting for transfers between devices, shards(): lax.all_to_all(attention_out[0], 'seq', split_axis=1, concat_axis=0, tile...  24.3 us
    all_to_all x1, waiting for transfers between devices, shards(): lax.all_to_all(query_rows[0], 'seq', split_axis=1, concat_axis=0, tiled=T...  21.8 us
    sub x2, other arithmetic, one_block(): weights = jnp.exp(scores - row_max)  15.4 us
  transfers between devices with their start and end apart: 17, of which 14 were waited for; matrix products, arithmetic and copies ran while one was open for 17% of the time, Pallas kernels for 0%

commit v1 on v0

--- a/solution.py
+++ b/solution.py
@@ -187,7 +187,9 @@
     )
     summed_out, summed_grad, summed_query = (
         lax.psum(partial_out.astype(jnp.bfloat16), "seq").astype(jnp.float32),
-        lax.psum(partial_grad.astype(jnp.bfloat16), "seq").astype(jnp.float32),
+        jnp.sum(lax.all_gather(partial_grad.astype(jnp.bfloat16), "seq"), axis=0).astype(
+            jnp.float32
+        ),
         lax.psum(partial_query.astype(jnp.bfloat16), "seq").astype(jnp.float32),
     )
     low_rank_output = summed_out.astype(jnp.bfloat16)

time: 588 us -> 529 us (0.90)
  waiting for transfers between devices: 329 us -> 273 us
    psum x1 -> x0, waiting for transfers between devices: 65.1 us -> none  [shards(): lax.psum(partial_grad.astype(jnp.bfloat16), 'seq').astype(jnp.float32)]
    all_gather x0 -> x1, waiting for transfers between devices: none -> 27.9 us  [shards(): lax.all_gather(partial_grad.astype(jnp.bfloat16), 'seq')]
    all_to_all x1, waiting for transfers between devices: 21.8 us -> 3.64 us  [shards(): lax.all_to_all(query_rows[0], 'seq', split_axis=1, concat_axis=0, tiled=T...]
    unnamed x71 -> x72, local copies, waits for them, and re-layouts: 28.1 us -> 26.2 us
  transfers between devices with their start and end apart: 17 -> 17, of which waited for: 14 -> 14; matrix products, arithmetic and copies ran while one was open for 17% -> 19% of each run, Pallas kernels for 0% -> 0%
where the time goes in v1:
time: 529 us; the launch traced here: 520 us
  waiting for transfers between devices  273 us (52%)
  matrix products  79 us (15%)
  local copies, waits for them, and re-layouts  65.8 us (12%)
  starting transfers between devices  55.7 us (11%)
  other arithmetic  24.3 us (5%)
  between operations  14.7 us (3%)
  loops' own time  7.5 us (1%)
    psum x1, waiting for transfers between devices, shards(): low_rank_back = lax.psum(partial_back.astype(jnp.bfloat16), 'seq')  70.4 us
    all_to_all x1, waiting for transfers between devices, shards(): lax.all_to_all(out_grad[0], 'seq', split_axis=1, concat_axis=0, tiled=True)  52.7 us
    all_to_all x1, waiting for transfers between devices, shards(): lax.all_to_all(layer_input[0], 'seq', split_axis=1, concat_axis=0, tiled=...  49 us
    all_gather x1, waiting for transfers between devices, shards(): lax.all_gather(partial_grad.astype(jnp.bfloat16), 'seq')  27.9 us
    unnamed x72, local copies, waits for them, and re-layouts  26.2 us
    all_to_all x1, waiting for transfers between devices, shards(): lax.all_to_all(attention_out[0], 'seq', split_axis=1, concat_axis=0, tile...  23.2 us
    sub x2, other arithmetic, one_block(): weights = jnp.exp(scores - row_max)  15.1 us
    dot_general x8, matrix products, contract_axes(): lax.dot_general(left_side, right_side, (((left_dim,), (right_dim,)), ((),...  14.3 us
  transfers between devices with their start and end apart: 17, of which 14 were waited for; matrix products, arithmetic and copies ran while one was open for 19% of the time, Pallas kernels for 0%

profile of v1, /device:TPU:0, one launch (start us, length us, event | category | flops | bytes accessed | tf_op | source)
XLA Modules:
  0.0 520.0 jit_solution(18015893713077555286)
XLA Ops:
  13.1 4.2 all-to-all-start.4
  20.1 6.7 %all-to-all-done.4 = bf16[4,2,64,512]{3,1,2,0:T(2,128)(2,1)} async-done(((bf16[4,2,64,512]{3,1,2,0:T(2,128)(2,1)}), bf16[4,2,64,512]{3,1,2,0:T(2,128)(2,1)}, u32[]{:S(2)}, u32[]{:S(2)}) %all-to-all-start.4) | async-done | bytes 524320 | tf_op jit(solution)/shard_map/all_to_all | solution.py:152
  43.0 5.4 %fusion.34 = bf16[4,2,64,1024]{3,0,1,2:T(4,128)(2,1)S(1)} fusion(f32[8,64,1024,1]{2,1,0,3:T(8,128)} %bitcast.196, f32[4,2,8]{2,1,0:T(2,128)S(1)} %convert_reduce_fusion.1), kind=kOutput, calls=%fused_computation.56 | convolution fusion | flops 50855936 | bytes 3145984 | tf_op jit(solution)/shard_map/mcl,lrw->mcrw/dot_general | solution.py:145
  50.2 7.2 %all-to-all-done.2 = bf16[4,2,64,1024]{3,1,2,0:T(2,128)(2,1)S(1)} async-done(((bf16[4,2,64,1024]{3,1,2,0:T(2,128)(2,1)}), bf16[4,2,64,1024]{3,1,2,0:T(2,128)(2,1)S(1)}, u32[]{:S(2)}, u32[]{:S(2)}) %all-to-all-start.2) | async-done | bytes 1048608 | tf_op jit(solution)/shard_map/all_to_all | solution.py:153
  58.4 4.2 all-to-all-start.8
  64.0 13.2 %all-to-all-done.8 = bf16[4,2,64,1024]{3,1,2,0:T(2,128)(2,1)} async-done(((bf16[4,2,64,1024]{3,1,2,0:T(2,128)(2,1)}), bf16[4,2,64,1024]{3,1,2,0:T(2,128)(2,1)}, u32[]{:S(2)}, u32[]{:S(2)}) %all-to-all-start.8) | async-done | bytes 1048608 | tf_op jit(solution)/shard_map/all_to_all | solution.py:150
  77.2 6.7 %all-to-all-start.10 = ((bf16[128,8,512]{0,2,1:T(8,128)(2,1)}), bf16[128,8,512]{0,2,1:T(8,128)(2,1)S(1)}, u32[]{:S(2)}, u32[]{:S(2)}) async-start(bf16[128,8,512]{0,2,1:T(8,128)(2,1)} %bitcast.60), calls=%async_computation.10 | async-start | bytes 2097152 | tf_op jit(solution)/shard_map/all_to_all | solution.py:118
  86.3 23.2 %all-to-all-done.10 = bf16[128,8,512]{0,2,1:T(8,128)(2,1)S(1)} async-done(((bf16[128,8,512]{0,2,1:T(8,128)(2,1)}), bf16[128,8,512]{0,2,1:T(8,128)(2,1)S(1)}, u32[]{:S(2)}, u32[]{:S(2)}) %all-to-all-start.10) | async-done | bytes 1048608 | tf_op jit(solution)/shard_map/all_to_all | solution.py:118
  119.1 52.7 %all-to-all-done.3 = bf16[128,8,1024]{0,2,1:T(8,128)(2,1)S(1)} async-done(((bf16[128,8,1024]{0,2,1:T(8,128)(2,1)}), bf16[128,8,1024]{0,2,1:T(8,128)(2,1)S(1)}, u32[]{:S(2)}, u32[]{:S(2)}) %all-to-all-start.3) | async-done | bytes 2097184 | tf_op jit(solution)/shard_map/all_to_all | solution.py:117
  173.0 4.3 all-to-all-start.6
  186.2 49.0 %all-to-all-done.6 = bf16[128,8,1024]{0,2,1:T(8,128)(2,1)} async-done(((bf16[128,8,1024]{0,2,1:T(8,128)(2,1)}), bf16[128,8,1024]{0,2,1:T(8,128)(2,1)}, u32[]{:S(2)}, u32[]{:S(2)}) %all-to-all-start.6) | async-done | bytes 2097184 | tf_op jit(solution)/shard_map/all_to_all | solution.py:116
  235.1 4.4 all-to-all-start
  265.5 4.3 all-to-all-start.1
  281.1 27.9 %all-gather.9.cloned.1.call-done = bf16[8192,64]{0,1:T(8,128)(2,1)} async-done(((bf16[1024,64]{0,1:T(8,128)(2,1)}), bf16[8192,64]{0,1:T(8,128)(2,1)}) %all-gather.9.cloned.1.call-update) | async-done | bytes 1048592 | tf_op jit(solution)/shard_map/all_gather | solution.py:190
  314.6 49.0 %while.12 = (s32[]{:T(128)}, bf16[2,512,4,128]{3,2,1,0:T(4,128)(2,1)}, s32[2]{0:T(128)S(1)}, bf16[1280,4,128]{2,0,1:T(8,128)(2,1)S(1)}, s32[1024]{0:T(1024)S(1)}...) while((s32[]{:T(128)}, ...), condition=%wide.region_11.13_spmd, body=%wide.region_7.12_spmd.sunk | while | flops 1230110720 | bytes 50923260 | solution.py:93
  318.3 5.0 fusion.110
  325.1 7.5 %fusion.111 = (f32[4,512]{1,0:T(4,128)S(1)}, f32[4,512,768]{2,1,0:T(8,128)S(1)}) fusion(f32[4,512,768]{2,1,0:T(8,128)} %fusion.110, pred[512,768]{1,0:T(8,128)(4,1)S(1)} %compare_and_fusion.4), kind=kOutput, calls=%fused_computation.142.clone.1 | output fusion | flops 9437951 | bytes 12984320 | tf_op jit(solution)/shard_map/while/body/eval_jaxpr/sub | solution.py:79
  342.8 5.0 fusion.110
  349.6 7.5 %fusion.111 = (f32[4,512]{1,0:T(4,128)S(1)}, f32[4,512,768]{2,1,0:T(8,128)S(1)}) fusion(f32[4,512,768]{2,1,0:T(8,128)} %fusion.110, pred[512,768]{1,0:T(8,128)(4,1)S(1)} %compare_and_fusion.4), kind=kOutput, calls=%fused_computation.142.clone.1 | output fusion | flops 9437951 | bytes 12984320 | tf_op jit(solution)/shard_map/while/body/eval_jaxpr/sub | solution.py:79
  367.0 70.4 %all-reduce.6.cloned.1.call-done = (bf16[1024,64]{0,1:T(8,128)(2,1)}, bf16[1024,64]{0,1:T(8,128)(2,1)}, bf16[1024,64]{0,1:T(8,128)(2,1)}) async-done(((bf16[1024,64]{0,1:T(8,128)(2,1)}, bf16[1024,64]{0,1:T(8,128)(2,1)}, bf16[1024,64]{0,1:T(8,128)(2,1)}), (bf16[1024,64]{0,1:T(8,128)(2,1)}, bf16[1024,64]{0,1:T(8,128)(2,1)}, bf16[1024,64]{0,1:T(8,128)(2,1)})) %all-reduce.6.cloned.1.call-update) | async-done | bytes 393232 | tf_op jit(solution)/shard_map/psum | solution.py:215
  452.3 4.3 all-to-all-done.9
  480.2 7.4 %all-to-all-done.12 = bf16[4,2,64,1024]{3,1,2,0:T(2,128)(2,1)S(1)} async-done(((bf16[4,2,64,1024]{3,1,2,0:T(2,128)(2,1)}), bf16[4,2,64,1024]{3,1,2,0:T(2,128)(2,1)S(1)}, u32[]{:S(2)}, u32[]{:S(2)}) %all-to-all-start.12) | async-done | bytes 1048608 | tf_op jit(solution)/shard_map/all_to_all | solution.py:252
  487.6 4.4 all-to-all-start.7
  506.5 4.3 convolution_bitcast_fusion.1
  (185 shorter events, 168.7 us)
Async XLA Ops:
  7.2 23.0 %copy-start = (f32[8,64,1024]{2,1,0:T(8,128)S(1)}, f32[8,64,1024]{2,1,0:T(8,128)}, u32[]{:S(2)}) copy-start(f32[8,64,1024]{2,1,0:T(8,128)} %param.31) | copy-start | bytes 6291460
  8.7 34.3 %copy-start.26 = (f32[4,2,8]{2,1,0:T(2,128)}, f32[4,2,8]{2,1,0:T(2,128)S(1)}, u32[]{:S(2)}) copy-start(f32[4,2,8]{2,1,0:T(2,128)S(1)} %convert_reduce_fusion.1) | copy-start | bytes 772
  13.1 13.7 %all-to-all-start.4 = ((bf16[4,2,64,512]{3,1,2,0:T(2,128)(2,1)}), bf16[4,2,64,512]{3,1,2,0:T(2,128)(2,1)}, u32[]{:S(2)}, u32[]{:S(2)}) async-start(bf16[4,2,64,512]{3,1,2,0:T(2,128)(2,1)} %copy.141), calls=%async_computation.4 | async-start | bytes 1048576 | tf_op jit(solution)/shard_map/all_to_all | solution.py:152
  26.7 12.3 %all-to-all-start.5 = ((bf16[4,2,64,512]{3,2,1,0:T(8,128)(2,1)}), bf16[4,2,64,512]{3,2,1,0:T(8,128)(2,1)S(1)}, u32[]{:S(2)}, u32[]{:S(2)}) async-start(bf16[4,2,64,512]{3,2,1,0:T(8,128)(2,1)} %copy.151), calls=%async_computation.5 | async-start | bytes 1048576 | tf_op jit(solution)/shard_map/all_to_all | solution.py:151
  39.0 18.4 %all-to-all-start.2 = ((bf16[4,2,64,1024]{3,1,2,0:T(2,128)(2,1)}), bf16[4,2,64,1024]{3,1,2,0:T(2,128)(2,1)S(1)}, u32[]{:S(2)}, u32[]{:S(2)}) async-start(bf16[4,2,64,1024]{3,1,2,0:T(2,128)(2,1)} %copy.134), calls=%async_computation.2 | async-start | bytes 2097152 | tf_op jit(solution)/shard_map/all_to_all | solution.py:153
  48.4 14.3 %copy-start.12 = (bf16[1,128,4096]{2,1,0:T(8,128)(2,1)S(1)}, bf16[1,128,4096]{2,1,0:T(8,128)(2,1)}, u32[]{:S(2)}) copy-start(bf16[1,128,4096]{2,1,0:T(8,128)(2,1)} %param.20) | copy-start | bytes 3145732
  58.4 18.8 %all-to-all-start.8 = ((bf16[4,2,64,1024]{3,1,2,0:T(2,128)(2,1)}), bf16[4,2,64,1024]{3,1,2,0:T(2,128)(2,1)}, u32[]{:S(2)}, u32[]{:S(2)}) async-start(bf16[4,2,64,1024]{3,1,2,0:T(2,128)(2,1)} %copy.162), calls=%async_computation.8 | async-start | bytes 2097152 | tf_op jit(solution)/shard_map/all_to_all | solution.py:150
  62.7 21.2 %copy-start.7 = (bf16[1,128,8192]{2,1,0:T(8,128)(2,1)S(1)}, bf16[1,128,8192]{2,1,0:T(8,128)(2,1)}, u32[]{:S(2)}) copy-start(bf16[1,128,8192]{2,1,0:T(8,128)(2,1)} %param.19) | copy-start | bytes 6291460
  77.2 32.4 %all-to-all-start.10 = ((bf16[128,8,512]{0,2,1:T(8,128)(2,1)}), bf16[128,8,512]{0,2,1:T(8,128)(2,1)S(1)}, u32[]{:S(2)}, u32[]{:S(2)}) async-start(bf16[128,8,512]{0,2,1:T(8,128)(2,1)} %bitcast.60), calls=%async_computation.10 | async-start | bytes 2097152 | tf_op jit(solution)/shard_map/all_to_all | solution.py:118
  110.5 61.2 %all-to-all-start.3 = ((bf16[128,8,1024]{0,2,1:T(8,128)(2,1)}), bf16[128,8,1024]{0,2,1:T(8,128)(2,1)S(1)}, u32[]{:S(2)}, u32[]{:S(2)}) async-start(bf16[128,8,1024]{0,2,1:T(8,128)(2,1)} %bitcast.189), calls=%async_computation.3 | async-start | bytes 4194304 | tf_op jit(solution)/shard_map/all_to_all | solution.py:117
  114.2 157.2 %all-gather.7.cloned.1.call-start = ((), (), s32[]{:S(2)}) async-start(), calls=%async_computation.13 | async-start | bytes 1179648 | tf_op jit(solution)/shard_map/all_gather | solution.py:126
  173.0 62.1 %all-to-all-start.6 = ((bf16[128,8,1024]{0,2,1:T(8,128)(2,1)}), bf16[128,8,1024]{0,2,1:T(8,128)(2,1)}, u32[]{:S(2)}, u32[]{:S(2)}) async-start(bf16[128,8,1024]{0,2,1:T(8,128)(2,1)} %bitcast.188), calls=%async_computation.6 | async-start | bytes 4194304 | tf_op jit(solution)/shard_map/all_to_all | solution.py:116
  177.4 95.8 %all-gather.11.cloned.1.call-start = ((), (), s32[]{:S(2)}) async-start(), calls=%async_computation.15 | async-start | bytes 1179648 | tf_op jit(solution)/shard_map/all_gather | solution.py:127
  235.1 30.4 %all-to-all-start = ((bf16[128,8,512]{0,2,1:T(8,128)(2,1)}), bf16[128,8,512]{0,2,1:T(8,128)(2,1)}, u32[]{:S(2)}, u32[]{:S(2)}) async-start(bf16[128,8,512]{0,2,1:T(8,128)(2,1)} %bitcast.10), calls=%async_computation | async-start | bytes 2097152 | tf_op jit(solution)/shard_map/all_to_all | solution.py:120
  239.6 69.5 %all-gather.9.cloned.1.call-start = ((), (), s32[]{:S(2)}) async-start(), calls=%async_computation.14 | async-start | bytes 1179648 | tf_op jit(solution)/shard_map/all_gather | solution.py:190
  265.5 46.1 %all-to-all-start.1 = ((bf16[128,8,512]{0,2,1:T(8,128)(2,1)}), bf16[128,8,512]{0,2,1:T(8,128)(2,1)}, u32[]{:S(2)}, u32[]{:S(2)}) async-start(bf16[128,8,512]{0,2,1:T(8,128)(2,1)} %bitcast.12), calls=%async_computation.1 | async-start | bytes 2097152 | tf_op jit(solution)/shard_map/all_to_all | solution.py:119
  269.8 167.6 %all-reduce.6.cloned.1.call-start = ((), (), s32[]{:S(2)}) async-start(), calls=%async_computation.16 | async-start | bytes 786432 | tf_op jit(solution)/shard_map/psum | solution.py:215
  281.1 30.5 %copy-start.23 = (bf16[8,64,512]{2,0,1:T(8,128)(2,1)S(1)}, bf16[8,64,512]{2,0,1:T(8,128)(2,1)}, u32[]{:S(2)}) copy-start(bf16[8,64,512]{2,0,1:T(8,128)(2,1)} %copy-done.22) | copy-start | bytes 1572868
  443.5 13.1 %all-to-all-start.9 = ((bf16[4,2,64,512]{3,1,2,0:T(2,128)(2,1)}), bf16[4,2,64,512]{3,1,2,0:T(2,128)(2,1)}, u32[]{:S(2)}, u32[]{:S(2)}) async-start(bf16[4,2,64,512]{3,1,2,0:T(2,128)(2,1)} %copy.166), calls=%async_computation.9 | async-start | bytes 1048576 | tf_op jit(solution)/shard_map/all_to_all | solution.py:238
  449.6 11.1 %copy-start.10 = (bf16[8,128,1024]{2,1,0:T(8,128)(2,1)S(1)}, bf16[8,128,1024]{2,1,0:T(8,128)(2,1)}, u32[]{:S(2)}) copy-start(bf16[8,128,1024]{2,1,0:T(8,128)(2,1)} %copy.138) | copy-start | bytes 6291460
  456.6 13.1 %all-to-all-start.11 = ((bf16[4,2,64,512]{3,1,2,0:T(2,128)(2,1)}), bf16[4,2,64,512]{3,1,2,0:T(2,128)(2,1)}, u32[]{:S(2)}, u32[]{:S(2)}) async-start(bf16[4,2,64,512]{3,1,2,0:T(2,128)(2,1)} %copy.172), calls=%async_computation.11 | async-start | bytes 1048576 | tf_op jit(solution)/shard_map/all_to_all | solution.py:245
  469.6 18.0 %all-to-all-start.12 = ((bf16[4,2,64,1024]{3,1,2,0:T(2,128)(2,1)}), bf16[4,2,64,1024]{3,1,2,0:T(2,128)(2,1)S(1)}, u32[]{:S(2)}, u32[]{:S(2)}) async-start(bf16[4,2,64,1024]{3,1,2,0:T(2,128)(2,1)} %copy.177), calls=%async_computation.12 | async-start | bytes 2097152 | tf_op jit(solution)/shard_map/all_to_all | solution.py:252
  478.4 13.6 %copy-start.27 = (f32[4,2,8]{2,1,0:T(2,128)S(1)}, f32[4,2,8]{2,1,0:T(2,128)}, u32[]{:S(2)}) copy-start(f32[4,2,8]{2,1,0:T(2,128)} %copy-done.26) | copy-start | bytes 772
  487.6 18.9 %all-to-all-start.7 = ((bf16[4,2,64,1024]{3,1,2,0:T(2,128)(2,1)}), bf16[4,2,64,1024]{3,1,2,0:T(2,128)(2,1)}, u32[]{:S(2)}, u32[]{:S(2)}) async-start(bf16[4,2,64,1024]{3,1,2,0:T(2,128)(2,1)} %copy.157), calls=%async_computation.7 | async-start | bytes 2097152 | tf_op jit(solution)/shard_map/all_to_all | solution.py:231
  (23 other events, 103.2 us)
Sparse Core Ops, SparseCore 0:
  117.0 61.5 all-gather.6
  180.7 61.1 all-gather.10
  260.7 48.3 all-gather.8
  367.1 70.1 all-reduce.5
